TPU v7x, 256 devices: a whole 4x4x8 slice. The times are simulated.
256 devices in a mesh: grp: 8 (over y, core), col: 32 (over x, z).
Axes of the slice: x: 4, y: 4, z: 8, core: 2. Of those that a mesh axis runs over, the one named last changes fastest.
Arguments:
- state: float32 [2, 64, 524288], P(None, None, ('grp', 'col')), may hold values from -6 to 6
- wind: float32 [2, 64, 524288], P(None, None, ('grp', 'col')), may hold values from -5 to 5
- live: int32 [8, 32], P('grp'), may hold values from 1 to 128, 2048 in all within a row
- w_first: bfloat16 [128, 1024], replicated, may hold values from -0.5 to 0.5
- b_first: float32 [1024], replicated, may hold values from -3 to 3
- w_second: bfloat16 [1024, 1024], replicated, may hold values from -0.1875 to 0.1875
- b_second: float32 [1024], replicated, may hold values from -3 to 3
- w_third: bfloat16 [1024, 128], replicated, may hold values from -0.1875 to 0.1875
- b_third: float32 [128], replicated, may hold values from -2 to 2
Outputs:
- updated: float32 [2, 64, 524288], P(None, None, ('grp', 'col'))
Inputs may be any that keep to these rules, and one draw needn't show every extreme that they name: `live`: the 32 counts of each group sum to 2048, and in each group some device holds exactly 128.
All inputs are finite; a program needn't handle non-finite values.
Results may differ from a plain program's by a relative error of at most 0.0023.
Values may be sent and summed in bfloat16 or wider, within the bound.
No kernel may reach another device: no remote copies, remote signals or barrier semaphores. Data moves between devices by JAX's collectives and lax.ppermute only.
A program may use at most 64 MiB of HBM per device.

v0:
```python
import functools

import jax
import jax.numpy as jnp
import numpy as np
from jax import lax
from jax.experimental import pallas as pl
from jax.experimental.pallas import tpu as pltpu
from jax.sharding import PartitionSpec as P

TIMESTEP = 0.1
LANES = 128
TILE = 512
CHUNK = 256
BF = jnp.bfloat16
F32 = jnp.float32
MIB = 2**20


def gll_table():
    points = np.array([-1.0, -1.0 / np.sqrt(5.0), 1.0 / np.sqrt(5.0), 1.0])
    legendre = 0.5 * (5.0 * points**3 - 3.0 * points)
    deriv_table = np.zeros((4, 4))
    for i in range(4):
        for j in range(4):
            if i != j:
                deriv_table[i, j] = legendre[i] / (legendre[j] * (points[i] - points[j]))
    deriv_table[0, 0] = -3.0
    deriv_table[3, 3] = 3.0
    return deriv_table


def deriv_operand():
    deriv_table = gll_table()
    along_xi = np.kron(np.eye(8), np.kron(np.eye(4), deriv_table)).T
    along_eta = np.kron(np.eye(8), np.kron(deriv_table, np.eye(4))).T
    both = np.concatenate([along_xi, along_eta], axis=1).astype(np.float32)
    high = both.astype(jnp.bfloat16)
    low = (both - high.astype(np.float32)).astype(jnp.bfloat16)
    return jnp.asarray(np.concatenate([high, high, low], axis=0))


def block_rate(s, wind_xi, wind_eta, deriv):
    high = s.astype(BF)
    low = (s - high.astype(F32)).astype(BF)
    d = jnp.dot(
        jnp.concatenate([high, low, high], axis=1), deriv, preferred_element_type=F32
    )
    return -(wind_xi * d[:, :LANES] + wind_eta * d[:, LANES:])


def both_fields(w):
    return jnp.concatenate([w, w], axis=0)


def lane_ids():
    return lax.broadcasted_iota(jnp.int32, (LANES, LANES), 1)


def own_live(live_ref):
    return live_ref[0, lax.axis_index("col")] * 16


def edge_kernel(live_ref, s_hbm, w_hbm, d_hbm, last_ref, first_ref, s_v, w_v, deriv, sems):
    start = own_live(live_ref) - 16
    block = pl.multiple_of(start // LANES * LANES, LANES)
    copies = [
        pltpu.make_async_copy(s_hbm.at[:, pl.ds(0, LANES)], s_v.at[0], sems.at[0]),
        pltpu.make_async_copy(w_hbm.at[:, pl.ds(0, LANES)], w_v.at[0], sems.at[1]),
        pltpu.make_async_copy(s_hbm.at[:, pl.ds(block, LANES)], s_v.at[1], sems.at[2]),
        pltpu.make_async_copy(w_hbm.at[:, pl.ds(block, LANES)], w_v.at[1], sems.at[3]),
        pltpu.make_async_copy(d_hbm, deriv, sems.at[4]),
    ]
    for copy in copies:
        copy.start()
    for copy in copies:
        copy.wait()
    rates = [
        block_rate(s_v[k], both_fields(w_v[k, 0:64]), both_fields(w_v[k, 64:128]), deriv[...])
        for k in range(2)
    ]
    rows = lax.broadcasted_iota(jnp.int32, (16, LANES), 0)
    turn = LANES - 3 - (start - block)
    east = pltpu.roll(rates[1], jnp.where(turn < 0, turn + LANES, turn), 1).T[0:16]
    last_ref[...] = jnp.where(rows % 4 == 0, east, 0.0)
    west = pltpu.roll(rates[0], 3, 1).T[0:16]
    first_ref[...] = jnp.where(rows % 4 == 3, west, 0.0)


def main_kernel(
    live_ref, s_hbm, w_hbm, w1_hbm, b1_hbm, w2_hbm, b2_hbm, w3_hbm, b3_hbm, d_hbm, o_hbm,
    s_v, w_v, w1, b1, w2, b2, w3, b3, deriv, w3t, h1, h2, rate, o_v, in_sems, out_sems,
):
    columns, units = h1.shape
    tiles = columns // TILE
    count = own_live(live_ref)

    def fetch(index, source, target):
        copy = pltpu.make_async_copy(source, target, in_sems.at[index])
        copy.start()
        return copy

    def cut(ref, tile):
        return ref.at[:, pl.ds(tile * TILE, TILE)]

    s_copies = [fetch(0, cut(s_hbm, 0), cut(s_v, 0))]
    early = [fetch(4, w1_hbm, w1), fetch(5, b1_hbm, b1)]
    s_copies += [fetch(t, cut(s_hbm, t), cut(s_v, t)) for t in range(1, tiles)]
    later = [
        fetch(6, w2_hbm, w2),
        fetch(7, b2_hbm, b2),
        fetch(8, w3_hbm, w3),
        fetch(9, b3_hbm, b3),
        fetch(10, d_hbm, deriv),
        fetch(11, w_hbm, w_v),
    ]
    for copy in early:
        copy.wait()
    for t in range(tiles):
        s_copies[t].wait()
        x = s_v[:, t * TILE : (t + 1) * TILE].astype(BF)
        for n in range(0, units, CHUNK):
            a = lax.dot_general(
                x, w1[:, n : n + CHUNK], (((0,), (0,)), ((), ())), preferred_element_type=F32
            )
            h1[t * TILE : (t + 1) * TILE, n : n + CHUNK] = jax.nn.silu(
                a + b1[:, n : n + CHUNK]
            ).astype(BF)
    for copy in later:
        copy.wait()
    w3t[...] = w3[...].T
    b3_rows = jnp.broadcast_to(b3[...], (LANES, LANES)).T
    for c in range(0, columns, LANES):
        cols = slice(c, c + LANES)
        rate[:, cols] = block_rate(
            s_v[:, cols], both_fields(w_v[0:64, cols]), both_fields(w_v[64:128, cols]), deriv[...]
        )
    lanes = lane_ids()
    outs = []
    for t in range(tiles):
        rows = slice(t * TILE, (t + 1) * TILE)
        for n in range(0, units, CHUNK):
            a = jnp.dot(h1[rows], w2[:, n : n + CHUNK], preferred_element_type=F32)
            h2[rows, n : n + CHUNK] = jax.nn.silu(a + b2[:, n : n + CHUNK]).astype(BF)
        third = lax.dot_general(
            w3t[...], h2[rows], (((1,), (1,)), ((), ())), preferred_element_type=F32
        )
        for c in range(t * TILE, (t + 1) * TILE, LANES):
            cols = slice(c, c + LANES)
            own = rate[:, cols]
            after = rate[:, c + LANES : c + 2 * LANES] if c + LANES < columns else own
            prior = rate[:, c - LANES : c] if c else own
            ids = lanes + c
            east = jnp.where(
                lanes < LANES - 13, pltpu.roll(own, LANES - 13, 1), pltpu.roll(after, LANES - 13, 1)
            )
            west = jnp.where(lanes >= 13, pltpu.roll(own, 13, 1), pltpu.roll(prior, 13, 1))
            east = jnp.where(ids < count - 16, east, 0.0)
            west = jnp.where(ids >= 16, west, 0.0)
            twin = jnp.where(lanes % 4 == 3, east, jnp.where(lanes % 4 == 0, west, own))
            k = c - t * TILE
            tendency = (third[:, k : k + LANES] + b3_rows).astype(BF).astype(F32)
            value = s_v[:, cols] + TIMESTEP * 0.5 * (own + twin) + tendency
            o_v[:, cols] = jnp.where(ids < count, value, 0.0)
        copy = pltpu.make_async_copy(cut(o_v, t), cut(o_hbm, t), out_sems.at[t])
        copy.start()
        outs.append(copy)
    for copy in outs:
        copy.wait()


def twin_kernel(live_ref, before_ref, after_ref, i_hbm, o_hbm, held, sems):
    del i_hbm
    start = own_live(live_ref) - 16
    block = pl.multiple_of(start // LANES * LANES, LANES)
    spots = [o_hbm.at[:, pl.ds(0, LANES)], o_hbm.at[:, pl.ds(block, LANES)]]
    loads = [pltpu.make_async_copy(spots[k], held.at[k], sems.at[k]) for k in range(2)]
    for copy in loads:
        copy.start()
    pad = jnp.zeros((LANES - 16, LANES), F32)
    half = 0.5 * TIMESTEP
    west = half * jnp.concatenate([before_ref[...], pad], axis=0).T
    east = half * pltpu.roll(jnp.concatenate([after_ref[...], pad], axis=0).T, start - block, 1)
    for copy in loads:
        copy.wait()
    shared = block == 0
    held[0] = held[0] + west + jnp.where(shared, east, 0.0)
    held[1] = held[1] + east + jnp.where(shared, west, 0.0)
    stores = [pltpu.make_async_copy(held.at[k], spots[k], sems.at[k]) for k in range(2)]
    stores[0].start()
    stores[0].wait()
    stores[1].start()
    stores[1].wait()


def passed_along(block, axis, distance):
    devices = range(lax.axis_size(axis))
    route = [((i - distance) % len(devices), i) for i in devices]
    return lax.ppermute(block, axis, route)


def body(state, wind, live, w_first, b_first, w_second, b_second, w_third, b_third):
    fields, levels, columns = state.shape
    features = fields * levels
    units = w_first.shape[1]
    s = state.reshape(features, columns)
    w = wind.reshape(features, columns)
    deriv = deriv_operand()
    smem = pl.BlockSpec(memory_space=pltpu.SMEM)
    vmem = pl.BlockSpec(memory_space=pltpu.VMEM)
    hbm = pl.BlockSpec(memory_space=pltpu.HBM)
    edge = jax.ShapeDtypeStruct((16, LANES), F32)
    last, first = pl.pallas_call(
        edge_kernel,
        out_shape=(edge, edge),
        in_specs=[smem, hbm, hbm, hbm],
        out_specs=(vmem, vmem),
        scratch_shapes=[
            pltpu.VMEM((2, features, LANES), F32),
            pltpu.VMEM((2, features, LANES), F32),
            pltpu.VMEM(deriv.shape, BF),
            pltpu.SemaphoreType.DMA((5,)),
        ],
        compiler_params=pltpu.CompilerParams(vmem_limit_bytes=62 * MIB),
        cost_estimate=pl.CostEstimate(flops=10**7, bytes_accessed=10**5, transcendentals=0),
    )(live, s, w, deriv)
    before = passed_along(last, ("grp", "col"), 1)
    after = passed_along(first, ("grp", "col"), -1)
    operands = [
        s, w, w_first, b_first[None], w_second, b_second[None], w_third, b_third[None], deriv
    ]
    out = pl.pallas_call(
        main_kernel,
        out_shape=jax.ShapeDtypeStruct((features, columns), F32),
        in_specs=[smem] + [hbm] * len(operands),
        out_specs=hbm,
        scratch_shapes=[pltpu.VMEM(a.shape, a.dtype) for a in operands]
        + [
            pltpu.VMEM((LANES, units), BF),
            pltpu.VMEM((columns, units), BF),
            pltpu.VMEM((columns, units), BF),
            pltpu.VMEM((features, columns), F32),
            pltpu.VMEM((features, columns), F32),
            pltpu.SemaphoreType.DMA((12,)),
            pltpu.SemaphoreType.DMA((columns // TILE,)),
        ],
        compiler_params=pltpu.CompilerParams(vmem_limit_bytes=62 * MIB),
        cost_estimate=pl.CostEstimate(
            flops=6 * 10**9, bytes_accessed=6 * 10**6, transcendentals=4 * 10**6
        ),
    )(live, *operands)
    out = pl.pallas_call(
        twin_kernel,
        out_shape=jax.ShapeDtypeStruct((features, columns), F32),
        in_specs=[smem, vmem, vmem, hbm],
        out_specs=hbm,
        scratch_shapes=[pltpu.VMEM((2, features, LANES), F32), pltpu.SemaphoreType.DMA((2,))],
        input_output_aliases={3: 0},
        compiler_params=pltpu.CompilerParams(vmem_limit_bytes=2 * MIB),
    )(live, before, after, out)
    return out.reshape(fields, levels, columns)


def solution(mesh):
    return jax.shard_map(
        body,
        mesh=mesh,
        in_specs=(
            P(None, None, ("grp", "col")),
            P(None, None, ("grp", "col")),
            P("grp", None),
            P(),
            P(),
            P(),
            P(),
            P(),
            P(),
        ),
        out_specs=P(None, None, ("grp", "col")),
        check_vma=False,
    )
```

profile of v0, /device:TPU:1, one launch (start us, length us, event | category | flops | bytes accessed | tf_op | source)
XLA Modules:
  0.0 26.0 jit_solution(2344827489928394393)
XLA Ops:
  0.0 2.7 %shard_map.100 = (f32[16,128]{1,0:T(8,128)}, f32[16,128]{1,0:T(8,128)}) custom-call(s32[1,32]{1,0:T(1,128)} %live_ref.5, f32[128,2048]{1,0:T(8,128)} %bitcast.6, f32[128,2048]{1,0:T(8,128)} %bitcast.8, bf16[384,256]{1,0:T(8,128)(2,1)} %constant.2.clone.d_hbm), custom_call_target="tpu_custom_call" | custom-call | flops 10000000 | bytes 100000 | tf_op jit(solution)/shard_map/pallas_call | solution.py:213
  2.7 2.5 %collective-permute-start = (f32[16,128]{1,0:T(8,128)}, f32[16,128]{1,0:T(8,128)S(1)}, u32[]{:S(2)}, u32[]{:S(2)}) collective-permute-start(f32[16,128]{1,0:T(8,128)} %get-tuple-element.7), channel_id=1, source_target_pairs={{255,0},{0,1},{1,2},{2,3},{3,4},{4,5},{5,6},{6,7},{7,8},{8,9},{9,1... | collective-permute-start | bytes 24584 | tf_op jit(solution)/shard_map/ppermute | solution.py:199
  5.3 6.8 %collective-permute-start.1 = (f32[16,128]{1,0:T(8,128)}, f32[16,128]{1,0:T(8,128)S(1)}, u32[]{:S(2)}, u32[]{:S(2)}) collective-permute-start(f32[16,128]{1,0:T(8,128)} %get-tuple-element.8), channel_id=1, source_target_pairs={{1,0},{2,1},{3,2},{4,3},{5,4},{6,5},{7,6},{8,7},{9,8},{10,9},{11,1... | collective-permute-start | bytes 24584 | tf_op jit(solution)/shard_map/ppermute | solution.py:199
  12.1 0.0 copy-start
  12.1 11.1 %shard_map.101.i_hbm = f32[128,2048]{1,0:T(8,128)} custom-call(s32[1,32]{1,0:T(1,128)} %live_ref.5, f32[128,2048]{1,0:T(8,128)} %bitcast.7, f32[128,2048]{1,0:T(8,128)} %bitcast.9, bf16[128,1024]{1,0:T(8,128)(2,1)} %w1_hbm.1, f32[1,1024]{1,0:T(1,128)} %bitcast.10, bf16[1024,1024]{1,0:T(8,128)(2,1)} %w2_hbm.1, f32[1,1024]{1,0:T(1,128)} %bitcast.11, ...), custom_call_target="tpu_custom_call" | custom-call | flops 6000000000 | bytes 6000000 | tf_op jit(solution)/shard_map/pallas_call | solution.py:232
  23.2 0.0 collective-permute-done.before_ref
  23.2 0.0 collective-permute-done.1.after_ref
  23.2 0.0 copy-done
  23.3 2.7 %shard_map.102 = f32[128,2048]{1,0:T(8,128)} custom-call(s32[1,32]{1,0:T(1,128)S(1)} %copy-done, f32[16,128]{1,0:T(8,128)S(1)} %collective-permute-done.before_ref, f32[16,128]{1,0:T(8,128)S(1)} %collective-permute-done.1.after_ref, f32[128,2048]{1,0:T(8,128)} %shard_map.101.i_hbm), custom_call_target="tpu_custom_call", output_to_operand_aliasing={{}: (3, {})} | custom-call | tf_op jit(solution)/shard_map/pallas_call | solution.py:252
Async XLA Ops:
  2.7 20.5 %collective-permute-start = (f32[16,128]{1,0:T(8,128)}, f32[16,128]{1,0:T(8,128)S(1)}, u32[]{:S(2)}, u32[]{:S(2)}) collective-permute-start(f32[16,128]{1,0:T(8,128)} %get-tuple-element.7), channel_id=1, source_target_pairs={{255,0},{0,1},{1,2},{2,3},{3,4},{4,5},{5,6},{6,7},{7,8},{8,9},{9,1... | collective-permute-start | bytes 24584 | tf_op jit(solution)/shard_map/ppermute | solution.py:199
  5.3 18.0 %collective-permute-start.1 = (f32[16,128]{1,0:T(8,128)}, f32[16,128]{1,0:T(8,128)S(1)}, u32[]{:S(2)}, u32[]{:S(2)}) collective-permute-start(f32[16,128]{1,0:T(8,128)} %get-tuple-element.8), channel_id=1, source_target_pairs={{1,0},{2,1},{3,2},{4,3},{5,4},{6,5},{7,6},{8,7},{9,8},{10,9},{11,1... | collective-permute-start | bytes 24584 | tf_op jit(solution)/shard_map/ppermute | solution.py:199
  12.1 11.2 %copy-start = (s32[1,32]{1,0:T(1,128)S(1)}, s32[1,32]{1,0:T(1,128)}, u32[]{:S(2)}) copy-start(s32[1,32]{1,0:T(1,128)} %live_ref.5) | copy-start | bytes 388
where the time goes:
time: 26.1 us; the launch traced here: 26 us
  Pallas kernels  16.6 us (64%)
  starting transfers between devices  9.33 us (36%)
    pallas_call x1, Pallas kernels, body(): pl.pallas_call(main_kernel, out_shape=jax.ShapeDtypeStruct((features, col...  11.1 us
    ppermute x2, starting transfers between devices, passed_along(): return lax.ppermute(block, axis, route)  9.33 us
    pallas_call x1, Pallas kernels, body(): pl.pallas_call(edge_kernel, out_shape=(edge, edge), in_specs=[smem, hbm,...  2.72 us
    pallas_call x1, Pallas kernels, body(): pl.pallas_call(twin_kernel, out_shape=jax.ShapeDtypeStruct((features, col...  2.72 us
  transfers between devices with their start and end apart: 2, of which 0 were waited for; matrix products, arithmetic and copies ran while one was open for 0% of the time, Pallas kernels for 43%

commit v1 on v0

--- a/solution.py
+++ b/solution.py
@@ -61,7 +61,11 @@
     return live_ref[0, lax.axis_index("col")] * 16
 
 
-def edge_kernel(live_ref, s_hbm, w_hbm, d_hbm, last_ref, first_ref, s_v, w_v, deriv, sems):
+def even_device():
+    return lax.axis_index("col") % 2 == 0
+
+
+def edge_kernel(live_ref, s_hbm, w_hbm, d_hbm, even_ref, odd_ref, s_v, w_v, deriv, sems):
     start = own_live(live_ref) - 16
     block = pl.multiple_of(start // LANES * LANES, LANES)
     copies = [
@@ -79,12 +83,15 @@
         block_rate(s_v[k], both_fields(w_v[k, 0:64]), both_fields(w_v[k, 64:128]), deriv[...])
         for k in range(2)
     ]
-    rows = lax.broadcasted_iota(jnp.int32, (16, LANES), 0)
+    lanes = lane_ids()
+    kept = (lanes < 16) & (lanes % 4 == 0)
     turn = LANES - 3 - (start - block)
-    east = pltpu.roll(rates[1], jnp.where(turn < 0, turn + LANES, turn), 1).T[0:16]
-    last_ref[...] = jnp.where(rows % 4 == 0, east, 0.0)
-    west = pltpu.roll(rates[0], 3, 1).T[0:16]
-    first_ref[...] = jnp.where(rows % 4 == 3, west, 0.0)
+    east = pltpu.roll(rates[1], jnp.where(turn < 0, turn + LANES, turn), 1)
+    last = jnp.where(kept, east, 0.0)
+    first = jnp.where(kept, rates[0], 0.0)
+    even = even_device()
+    even_ref[...] = jnp.where(even, last, first)
+    odd_ref[...] = jnp.where(even, first, last)
 
 
 def main_kernel(
@@ -155,12 +162,14 @@
                 lanes < LANES - 13, pltpu.roll(own, LANES - 13, 1), pltpu.roll(after, LANES - 13, 1)
             )
             west = jnp.where(lanes >= 13, pltpu.roll(own, 13, 1), pltpu.roll(prior, 13, 1))
-            east = jnp.where(ids < count - 16, east, 0.0)
-            west = jnp.where(ids >= 16, west, 0.0)
-            twin = jnp.where(lanes % 4 == 3, east, jnp.where(lanes % 4 == 0, west, own))
+            pair = jnp.where(
+                lanes % 4 == 3,
+                jnp.where(ids < count - 16, own + east, 0.0),
+                jnp.where(lanes % 4 == 0, jnp.where(ids >= 16, own + west, 0.0), own + own),
+            )
             k = c - t * TILE
             tendency = (third[:, k : k + LANES] + b3_rows).astype(BF).astype(F32)
-            value = s_v[:, cols] + TIMESTEP * 0.5 * (own + twin) + tendency
+            value = s_v[:, cols] + TIMESTEP * 0.5 * pair + tendency
             o_v[:, cols] = jnp.where(ids < count, value, 0.0)
         copy = pltpu.make_async_copy(cut(o_v, t), cut(o_hbm, t), out_sems.at[t])
         copy.start()
@@ -169,34 +178,43 @@
         copy.wait()
 
 
-def twin_kernel(live_ref, before_ref, after_ref, i_hbm, o_hbm, held, sems):
+def twin_kernel(live_ref, even_hbm, odd_hbm, i_hbm, o_hbm, even_ref, odd_ref, held, sems):
     del i_hbm
     start = own_live(live_ref) - 16
     block = pl.multiple_of(start // LANES * LANES, LANES)
     spots = [o_hbm.at[:, pl.ds(0, LANES)], o_hbm.at[:, pl.ds(block, LANES)]]
-    loads = [pltpu.make_async_copy(spots[k], held.at[k], sems.at[k]) for k in range(2)]
+    loads = [
+        pltpu.make_async_copy(even_hbm, even_ref, sems.at[2]),
+        pltpu.make_async_copy(odd_hbm, odd_ref, sems.at[3]),
+        pltpu.make_async_copy(spots[0], held.at[0], sems.at[0]),
+        pltpu.make_async_copy(spots[1], held.at[1], sems.at[1]),
+    ]
     for copy in loads:
         copy.start()
-    pad = jnp.zeros((LANES - 16, LANES), F32)
+    for copy in loads:
+        copy.wait()
+    even = even_device()
     half = 0.5 * TIMESTEP
-    west = half * jnp.concatenate([before_ref[...], pad], axis=0).T
-    east = half * pltpu.roll(jnp.concatenate([after_ref[...], pad], axis=0).T, start - block, 1)
-    for copy in loads:
-        copy.wait()
+    west = half * jnp.where(even, odd_ref[...], even_ref[...])
+    east = half * pltpu.roll(jnp.where(even, even_ref[...], odd_ref[...]), start - block + 3, 1)
     shared = block == 0
     held[0] = held[0] + west + jnp.where(shared, east, 0.0)
     held[1] = held[1] + east + jnp.where(shared, west, 0.0)
     stores = [pltpu.make_async_copy(held.at[k], spots[k], sems.at[k]) for k in range(2)]
     stores[0].start()
+
+    @pl.when(block > 0)
+    def _():
+        stores[1].start()
+        stores[1].wait()
+
     stores[0].wait()
-    stores[1].start()
-    stores[1].wait()
-
-
-def passed_along(block, axis, distance):
-    devices = range(lax.axis_size(axis))
-    route = [((i - distance) % len(devices), i) for i in devices]
-    return lax.ppermute(block, axis, route)
+
+
+def pair_sum(block, axis, offset):
+    devices = lax.axis_size(axis)
+    pairs = [[i, (i + 1) % devices] for i in range(offset, devices, 2)]
+    return lax.psum(block, axis, axis_index_groups=pairs)
 
 
 def body(state, wind, live, w_first, b_first, w_second, b_second, w_third, b_third):
@@ -209,8 +227,8 @@
     smem = pl.BlockSpec(memory_space=pltpu.SMEM)
     vmem = pl.BlockSpec(memory_space=pltpu.VMEM)
     hbm = pl.BlockSpec(memory_space=pltpu.HBM)
-    edge = jax.ShapeDtypeStruct((16, LANES), F32)
-    last, first = pl.pallas_call(
+    edge = jax.ShapeDtypeStruct((features, LANES), F32)
+    even, odd = pl.pallas_call(
         edge_kernel,
         out_shape=(edge, edge),
         in_specs=[smem, hbm, hbm, hbm],
@@ -224,8 +242,8 @@
         compiler_params=pltpu.CompilerParams(vmem_limit_bytes=62 * MIB),
         cost_estimate=pl.CostEstimate(flops=10**7, bytes_accessed=10**5, transcendentals=0),
     )(live, s, w, deriv)
-    before = passed_along(last, ("grp", "col"), 1)
-    after = passed_along(first, ("grp", "col"), -1)
+    even = pair_sum(even, ("grp", "col"), 0)
+    odd = pair_sum(odd, ("grp", "col"), 1)
     operands = [
         s, w, w_first, b_first[None], w_second, b_second[None], w_third, b_third[None], deriv
     ]
@@ -252,12 +270,17 @@
     out = pl.pallas_call(
         twin_kernel,
         out_shape=jax.ShapeDtypeStruct((features, columns), F32),
-        in_specs=[smem, vmem, vmem, hbm],
+        in_specs=[smem, hbm, hbm, hbm],
         out_specs=hbm,
-        scratch_shapes=[pltpu.VMEM((2, features, LANES), F32), pltpu.SemaphoreType.DMA((2,))],
+        scratch_shapes=[
+            pltpu.VMEM(even.shape, F32),
+            pltpu.VMEM(odd.shape, F32),
+            pltpu.VMEM((2, features, LANES), F32),
+            pltpu.SemaphoreType.DMA((4,)),
+        ],
         input_output_aliases={3: 0},
-        compiler_params=pltpu.CompilerParams(vmem_limit_bytes=2 * MIB),
-    )(live, before, after, out)
+        compiler_params=pltpu.CompilerParams(vmem_limit_bytes=62 * MIB),
+    )(live, even, odd, out)
     return out.reshape(fields, levels, columns)
 
 

time: 26.1 us -> 94.3 us (3.61)
  waiting for transfers between devices: 0.01 us -> 64.5 us
  between operations: 0.04 us -> 13.4 us
  starting transfers between devices: 9.33 us -> 0.04 us
    psum x0 -> x2, waiting for transfers between devices: none -> 63.8 us  [pair_sum(): return lax.psum(block, axis, axis_index_groups=pairs)]
    ppermute x2 -> x0, starting transfers between devices: 9.33 us -> none  [passed_along(): return lax.ppermute(block, axis, route)]
  transfers between devices with their start and end apart: 2 -> 2, of which waited for: 0 -> 2; matrix products, arithmetic and copies ran while one was open for 0% -> 0% of each run, Pallas kernels for 43% -> 12%
where the time goes in v1:
time: 94.3 us; the launch traced here: 94.1 us
  waiting for transfers between devices  64.5 us (68%)
  Pallas kernels  16.1 us (17%)
  between operations  13.4 us (14%)
    psum x2, waiting for transfers between devices, pair_sum(): return lax.psum(block, axis, axis_index_groups=pairs)  63.8 us
    pallas_call x1, Pallas kernels, body(): pl.pallas_call(main_kernel, out_shape=jax.ShapeDtypeStruct((features, col...  11 us
    pallas_call x1, Pallas kernels, body(): pl.pallas_call(edge_kernel, out_shape=(edge, edge), in_specs=[smem, hbm,...  2.72 us
    pallas_call x1, Pallas kernels, body(): pl.pallas_call(twin_kernel, out_shape=jax.ShapeDtypeStruct((features, col...  2.38 us
  transfers between devices with their start and end apart: 2, of which 2 were waited for; matrix products, arithmetic and copies ran while one was open for 0% of the time, Pallas kernels for 12%

profile of v1, /device:TPU:1, one launch (start us, length us, event | category | flops | bytes accessed | tf_op | source)
XLA Modules:
  0.0 94.1 jit_solution(11224190028759315232)
XLA Ops:
  6.5 0.0 all-reduce.3.cloned.1.call-start
  6.5 2.7 %shard_map.100 = (f32[128,128]{1,0:T(8,128)}, f32[128,128]{1,0:T(8,128)}) custom-call(s32[1,32]{1,0:T(1,128)} %live_ref.5, f32[128,2048]{1,0:T(8,128)} %bitcast.6, f32[128,2048]{1,0:T(8,128)} %bitcast.8, bf16[384,256]{1,0:T(8,128)(2,1)} %constant.2.clone.d_hbm), custom_call_target="tpu_custom_call" | custom-call | flops 10000000 | bytes 100000 | tf_op jit(solution)/shard_map/pallas_call | solution.py:231
  9.3 0.0 all-reduce.3.cloned.1.call-update
  9.3 0.0 all-reduce.5.cloned.1.call-start
  9.3 0.7 all-reduce.5.cloned.1.call-update
  10.0 11.0 %shard_map.101.i_hbm = f32[128,2048]{1,0:T(8,128)} custom-call(s32[1,32]{1,0:T(1,128)} %live_ref.5, f32[128,2048]{1,0:T(8,128)} %bitcast.7, f32[128,2048]{1,0:T(8,128)} %bitcast.9, bf16[128,1024]{1,0:T(8,128)(2,1)} %w1_hbm.1, f32[1,1024]{1,0:T(1,128)} %bitcast.10, bf16[1024,1024]{1,0:T(8,128)(2,1)} %w2_hbm.1, f32[1,1024]{1,0:T(1,128)} %bitcast.11, ...), custom_call_target="tpu_custom_call" | custom-call | flops 6000000000 | bytes 6000000 | tf_op jit(solution)/shard_map/pallas_call | solution.py:250
  21.1 24.3 %all-reduce.3.cloned.1.call-done.even_hbm = f32[128,128]{1,0:T(8,128)} async-done(((f32[128,128]{1,0:T(8,128)}), f32[128,128]{1,0:T(8,128)}) %all-reduce.3.cloned.1.call-update) | async-done | bytes 65552 | tf_op jit(solution)/shard_map/psum | solution.py:217
  45.4 39.5 %all-reduce.5.cloned.1.call-done.odd_hbm = f32[128,128]{1,0:T(8,128)} async-done(((f32[128,128]{1,0:T(8,128)}), f32[128,128]{1,0:T(8,128)}) %all-reduce.5.cloned.1.call-update) | async-done | bytes 65552 | tf_op jit(solution)/shard_map/psum | solution.py:217
  84.9 2.4 %shard_map.102 = f32[128,2048]{1,0:T(8,128)} custom-call(s32[1,32]{1,0:T(1,128)} %live_ref.5, f32[128,128]{1,0:T(8,128)} %all-reduce.3.cloned.1.call-done.even_hbm, f32[128,128]{1,0:T(8,128)} %all-reduce.5.cloned.1.call-done.odd_hbm, f32[128,2048]{1,0:T(8,128)} %shard_map.101.i_hbm), custom_call_target="tpu_custom_call", output_to_operand_aliasing={{}: (3, {})} | custom-call | tf_op jit(solution)/shard_map/pallas_call | solution.py:270
Async XLA Ops:
  6.5 38.8 %all-reduce.3.cloned.1.call-start = ((), (), s32[]{:S(2)}) async-start(), calls=%async_computation | async-start | bytes 131072 | tf_op jit(solution)/shard_map/psum | solution.py:217
  9.3 75.6 %all-reduce.5.cloned.1.call-start = ((), (), s32[]{:S(2)}) async-start(), calls=%async_computation.1 | async-start | bytes 131072 | tf_op jit(solution)/shard_map/psum | solution.py:217
Sparse Core Ops, SparseCore 0:
  9.9 35.4 all-reduce.2
  47.9 36.9 all-reduce.4

commit v2 on v0

v2 whole, which is shorter than its diff:
```python
import functools

import jax
import jax.numpy as jnp
import numpy as np
from jax import lax
from jax.experimental import pallas as pl
from jax.experimental.pallas import tpu as pltpu
from jax.sharding import PartitionSpec as P

TIMESTEP = 0.1
LANES = 128
TILE = 512
EARLY = ((3, 2, 2, 1, 1, 0, 0, 0), (2, 1, 1, 0, 0, 0, 0, 0))
CHUNK = 256
BF = jnp.bfloat16
F32 = jnp.float32
MIB = 2**20


def gll_table():
    points = np.array([-1.0, -1.0 / np.sqrt(5.0), 1.0 / np.sqrt(5.0), 1.0])
    legendre = 0.5 * (5.0 * points**3 - 3.0 * points)
    deriv_table = np.zeros((4, 4))
    for i in range(4):
        for j in range(4):
            if i != j:
                deriv_table[i, j] = legendre[i] / (legendre[j] * (points[i] - points[j]))
    deriv_table[0, 0] = -3.0
    deriv_table[3, 3] = 3.0
    return deriv_table


def deriv_operand():
    deriv_table = gll_table()
    along_xi = np.kron(np.eye(8), np.kron(np.eye(4), deriv_table)).T
    along_eta = np.kron(np.eye(8), np.kron(deriv_table, np.eye(4))).T
    both = np.concatenate([along_xi, along_eta], axis=1).astype(np.float32)
    high = both.astype(jnp.bfloat16)
    low = (both - high.astype(np.float32)).astype(jnp.bfloat16)
    return jnp.asarray(np.concatenate([high, high, low], axis=0))


def block_rate(s, wind_xi, wind_eta, deriv):
    high = s.astype(BF)
    low = (s - high.astype(F32)).astype(BF)
    d = jnp.dot(
        jnp.concatenate([high, low, high], axis=1), deriv, preferred_element_type=F32
    )
    return -(wind_xi * d[:, :LANES] + wind_eta * d[:, LANES:])


def both_fields(w):
    return jnp.concatenate([w, w], axis=0)


def lane_ids():
    return lax.broadcasted_iota(jnp.int32, (LANES, LANES), 1)


def own_live(live_ref):
    return live_ref[0, lax.axis_index("col")] * 16


def early_tiles():
    col = lax.axis_index("col")
    amount = 0
    for z in range(8):
        here = jnp.where(col // 8 == 0, EARLY[0][z], EARLY[1][z])
        amount = jnp.where(col % 8 == z, here, amount)
    return amount


def fetch(source, target, sems, index):
    copy = pltpu.make_async_copy(source, target, sems.at[index])
    copy.start()
    return copy


def edge_fetches(live_ref, s_hbm, w_hbm, d_hbm, deriv, s_v, w_v, sems):
    start = own_live(live_ref) - 16
    block = pl.multiple_of(start // LANES * LANES, LANES)
    return [
        fetch(s_hbm.at[:, pl.ds(0, LANES)], s_v.at[0], sems, 0),
        fetch(w_hbm.at[:, pl.ds(0, LANES)], w_v.at[0], sems, 1),
        fetch(s_hbm.at[:, pl.ds(block, LANES)], s_v.at[1], sems, 2),
        fetch(w_hbm.at[:, pl.ds(block, LANES)], w_v.at[1], sems, 3),
        fetch(d_hbm, deriv, sems, 4),
    ]


def edge_rates(copies, live_ref, deriv, s_v, w_v):
    start = own_live(live_ref) - 16
    block = start // LANES * LANES
    for copy in copies:
        copy.wait()
    turn = jnp.where(start > block, LANES - (start - block), 0)
    lanes = lane_ids()

    def joined(first, last):
        return jnp.where(lanes < 16, first, pltpu.roll(last, lax.rem(turn + 16, LANES), 1))

    s = joined(s_v[0], s_v[1])
    w = joined(w_v[0], w_v[1])
    rate = block_rate(s, both_fields(w[0:64]), both_fields(w[64:128]), deriv[...])
    turned = rate.T
    rows = lax.broadcasted_iota(jnp.int32, (16, LANES), 0)
    east = pltpu.roll(turned[16:32], 13, 0)
    west = pltpu.roll(turned[0:16], 3, 0)
    return jnp.where(rows % 4 == 0, east, 0.0), jnp.where(rows % 4 == 3, west, 0.0)


def network_parts(hbm, vmem, sems, first_sem):
    return [fetch(a, b, sems, first_sem + k) for k, (a, b) in enumerate(zip(hbm, vmem))]


def columns_at(tile, size=TILE):
    return pl.ds(pl.multiple_of(tile * size, size), size)


def first_layer(tile, s_v, w1, b1, h1, size=TILE):
    units = h1.shape[1]
    x = s_v[:, columns_at(tile, size)].astype(BF)
    for n in range(0, units, CHUNK):
        a = lax.dot_general(
            x, w1[:, n : n + CHUNK], (((0,), (0,)), ((), ())), preferred_element_type=F32
        )
        h1[columns_at(tile, size), n : n + CHUNK] = jax.nn.silu(a + b1[:, n : n + CHUNK]).astype(BF)


def rate_at(block, s_v, w_v, deriv, rate, slot):
    cols = pl.ds(pl.multiple_of(block * LANES, LANES), LANES)
    rate[:, pl.ds(pl.multiple_of(slot * LANES + LANES, LANES), LANES)] = block_rate(
        s_v[:, cols], both_fields(w_v[0:64, cols]), both_fields(w_v[64:128, cols]), deriv[...]
    )


def finish_tile(tile, count, s_v, w2, b2, w3t, b3_rows, h1, h2, rate, o_v, size=TILE):
    units = h1.shape[1]
    h = h1[columns_at(tile, size), :]
    for n in range(0, units, CHUNK):
        a = jnp.dot(h, w2[:, n : n + CHUNK], preferred_element_type=F32)
        h2[0:size, n : n + CHUNK] = jax.nn.silu(a + b2[:, n : n + CHUNK]).astype(BF)
    third = lax.dot_general(
        w3t[...], h2[0:size], (((1,), (1,)), ((), ())), preferred_element_type=F32
    )
    lanes = lane_ids()
    for k in range(0, size, LANES):
        base = pl.multiple_of(tile * size + k, LANES)
        own = rate[:, pl.ds(base + LANES, LANES)]
        after = rate[:, pl.ds(base + 2 * LANES, LANES)]
        prior = rate[:, pl.ds(base, LANES)]
        ids = lanes + base
        east = pltpu.roll(jnp.where(lanes < 13, after, own), LANES - 13, 1)
        west = pltpu.roll(jnp.where(lanes >= LANES - 13, prior, own), 13, 1)
        east = jnp.where(ids < count - 16, east, 0.0)
        west = jnp.where(ids >= 16, west, 0.0)
        twin = jnp.where(lanes % 4 == 3, east, jnp.where(lanes % 4 == 0, west, own))
        tendency = (third[:, k : k + LANES] + b3_rows[...]).astype(BF).astype(F32)
        value = s_v[:, pl.ds(base, LANES)] + (0.5 * TIMESTEP) * (own + twin) + tendency
        o_v[:, pl.ds(base, LANES)] = jnp.where(ids < count, value, 0.0)


def ready_last(w3, b3, w3t, b3_rows):
    w3t[...] = w3[...].T
    b3_rows[...] = jnp.broadcast_to(b3[...], (LANES, LANES)).T


def do_tiles(tiles, count, begun, refs, o_hbm, sem):
    s_v, w1, b1, w2, b2, w3, b3, deriv, w_v, w3t, b3_rows, h1, h2, rate, o_v = refs
    for copy in begun[:3]:
        copy.wait()
    for tile in tiles:
        first_layer(tile, s_v, w1, b1, h1)
    for copy in begun[3:]:
        copy.wait()
    ready_last(w3, b3, w3t, b3_rows)
    per = TILE // LANES
    for block in range(max(tiles[0] * per - 1, 0), min(tiles[-1] * per + per + 1, s_v.shape[1] // LANES)):
        rate_at(block, s_v, w_v, deriv, rate, block)

    def out_copy(tile):
        cols = columns_at(tile)
        return pltpu.make_async_copy(o_v.at[:, cols], o_hbm.at[:, cols], sem)

    for tile in tiles:
        finish_tile(tile, count, s_v, w2, b2, w3t, b3_rows, h1, h2, rate, o_v)
        out_copy(tile).start()
    for tile in tiles:
        out_copy(tile).wait()


def edge_kernel(live_ref, s_hbm, w_hbm, d_hbm, last_ref, first_ref, s_e, w_e, deriv, sems):
    copies = edge_fetches(live_ref, s_hbm, w_hbm, d_hbm, deriv, s_e, w_e, sems)
    last_ref[...], first_ref[...] = edge_rates(copies, live_ref, deriv, s_e, w_e)


def early_kernel(
    live_ref, first_ref, s_v, w_v, w1, b1, w2, b2, w3, b3, deriv, passed_ref, o_hbm,
    w3t, b3_rows, h1, h2, rate, o_v, sems,
):
    early = early_tiles()
    refs = [s_v, w1, b1, w2, b2, w3, b3, deriv, w_v, w3t, b3_rows, h1, h2, rate, o_v]
    for amount in sorted(set(EARLY[0] + EARLY[1]) - {0}):

        @pl.when(early == amount)
        def _():
            do_tiles(range(amount), own_live(live_ref), [], refs, o_hbm, sems.at[0])

    passed_ref[...] = first_ref[...]


def late_kernel(
    live_ref, s_v, w_v, w1, b1, w2, b2, w3, b3, deriv, i_hbm, o_hbm,
    w3t, b3_rows, h1, h2, rate, o_v, sems,
):
    del i_hbm
    early = early_tiles()
    refs = [s_v, w1, b1, w2, b2, w3, b3, deriv, w_v, w3t, b3_rows, h1, h2, rate, o_v]
    tiles = s_v.shape[1] // TILE
    for amount in sorted(set(EARLY[0] + EARLY[1]) | {0}):

        @pl.when(early == amount)
        def _():
            do_tiles(range(amount, tiles), own_live(live_ref), [], refs, o_hbm, sems.at[0])


def twin_kernel(live_ref, after_ref, before_ref, i_hbm, o_hbm, held, sems):
    del i_hbm
    start = own_live(live_ref) - 16
    block = pl.multiple_of(start // LANES * LANES, LANES)
    spots = [o_hbm.at[:, pl.ds(0, LANES)], o_hbm.at[:, pl.ds(block, LANES)]]
    loads = [pltpu.make_async_copy(spots[k], held.at[k], sems.at[k]) for k in range(2)]
    for copy in loads:
        copy.start()
    pad = jnp.zeros((LANES - 16, LANES), F32)
    half = 0.5 * TIMESTEP
    west = half * jnp.concatenate([before_ref[...], pad], axis=0).T
    east = half * pltpu.roll(jnp.concatenate([after_ref[...], pad], axis=0).T, start - block, 1)
    for copy in loads:
        copy.wait()
    shared = block == 0
    held[0] = held[0] + west + jnp.where(shared, east, 0.0)
    held[1] = held[1] + east + jnp.where(shared, west, 0.0)
    stores = [pltpu.make_async_copy(held.at[k], spots[k], sems.at[k]) for k in range(2)]
    stores[0].start()

    @pl.when(block > 0)
    def _():
        stores[1].start()
        stores[1].wait()

    stores[0].wait()


def passed_along(block, axis, distance):
    devices = range(lax.axis_size(axis))
    route = [((i - distance) % len(devices), i) for i in devices]
    return lax.ppermute(block, axis, route)


def body(state, wind, live, w_first, b_first, w_second, b_second, w_third, b_third):
    fields, levels, columns = state.shape
    features = fields * levels
    units = w_first.shape[1]
    s = state.reshape(features, columns)
    w = wind.reshape(features, columns)
    deriv = deriv_operand()
    smem = pl.BlockSpec(memory_space=pltpu.SMEM)
    vmem = pl.BlockSpec(memory_space=pltpu.VMEM)
    hbm = pl.BlockSpec(memory_space=pltpu.HBM)
    edge = jax.ShapeDtypeStruct((16, LANES), F32)
    whole = jax.ShapeDtypeStruct((features, columns), F32)
    operands = [
        s, w, w_first, b_first[None], w_second, b_second[None], w_third, b_third[None], deriv
    ]
    work = [
        pltpu.VMEM((LANES, units), BF),
        pltpu.VMEM((LANES, LANES), F32),
        pltpu.VMEM((columns, units), BF),
        pltpu.VMEM((TILE, units), BF),
        pltpu.VMEM((features, columns + 2 * LANES), F32),
        pltpu.VMEM((features, columns), F32),
    ]
    pair = pltpu.VMEM((2, features, LANES), F32)
    last, first = pl.pallas_call(
        edge_kernel,
        out_shape=(edge, edge),
        in_specs=[smem, hbm, hbm, hbm],
        out_specs=(vmem, vmem),
        scratch_shapes=[pair, pair, pltpu.VMEM(deriv.shape, BF), pltpu.SemaphoreType.DMA((5,))],
        compiler_params=pltpu.CompilerParams(vmem_limit_bytes=54 * MIB),
        cost_estimate=pl.CostEstimate(flops=4 * 10**9, bytes_accessed=10**5, transcendentals=0),
    )(live, s, w, deriv)
    before = passed_along(last, ("grp", "col"), 1)
    work.append(pltpu.SemaphoreType.DMA((1,)))
    params = pltpu.CompilerParams(vmem_limit_bytes=28 * MIB)
    first, out = pl.pallas_call(
        early_kernel,
        out_shape=(edge, whole),
        in_specs=[smem, vmem] + [vmem] * len(operands),
        out_specs=(vmem, hbm),
        scratch_shapes=work,
        compiler_params=params,
    )(live, first, *operands)
    after = passed_along(first, ("grp", "col"), -1)
    out = pl.pallas_call(
        late_kernel,
        out_shape=whole,
        in_specs=[smem] + [vmem] * len(operands) + [hbm],
        out_specs=hbm,
        scratch_shapes=work,
        input_output_aliases={1 + len(operands): 0},
        compiler_params=params,
        cost_estimate=pl.CostEstimate(
            flops=6 * 10**9, bytes_accessed=6 * 10**6, transcendentals=4 * 10**6
        ),
    )(live, *operands, out)
    out = pl.pallas_call(
        twin_kernel,
        out_shape=whole,
        in_specs=[smem, vmem, vmem, hbm],
        out_specs=hbm,
        scratch_shapes=[pair, pltpu.SemaphoreType.DMA((2,))],
        input_output_aliases={3: 0},
        compiler_params=pltpu.CompilerParams(vmem_limit_bytes=2 * MIB),
    )(live, after, before, out)
    return out.reshape(fields, levels, columns)


def solution(mesh):
    return jax.shard_map(
        body,
        mesh=mesh,
        in_specs=(
            P(None, None, ("grp", "col")),
            P(None, None, ("grp", "col")),
            P("grp", None),
            P(),
            P(),
            P(),
            P(),
            P(),
            P(),
        ),
        out_specs=P(None, None, ("grp", "col")),
        check_vma=False,
    )
```

time: 26.1 us -> 21.7 us (0.83)
  the two profiles are of different devices: /device:TPU:1 before, /device:TPU:40 now
where the time goes in v2:
time: 21.7 us; the launch traced here: 21.5 us
  Pallas kernels  16.4 us (76%)
  starting transfers between devices  4.09 us (19%)
  local copies, waits for them, and re-layouts  0.74 us (3%)
  between operations  0.34 us (2%)
    pallas_call x1, Pallas kernels, body(): pl.pallas_call(late_kernel, out_shape=whole, in_specs=[smem] + [vmem] * l...  5.73 us
    pallas_call x1, Pallas kernels, body(): pl.pallas_call(early_kernel, out_shape=(edge, whole), in_specs=[smem, vme...  5.31 us
    ppermute x2, starting transfers between devices, passed_along(): return lax.ppermute(block, axis, route)  4.09 us
    pallas_call x1, Pallas kernels, body(): pl.pallas_call(edge_kernel, out_shape=(edge, edge), in_specs=[smem, hbm,...  3.2 us
    pallas_call x1, Pallas kernels, body(): pl.pallas_call(twin_kernel, out_shape=whole, in_specs=[smem, vmem, vmem,...  2.13 us
    unnamed x22, local copies, waits for them, and re-layouts  0.74 us
  transfers between devices with their start and end apart: 2, of which 0 were waited for; matrix products, arithmetic and copies ran while one was open for 0% of the time, Pallas kernels for 51%

profile of v2, /device:TPU:40, one launch (start us, length us, event | category | flops | bytes accessed | tf_op | source)
XLA Modules:
  0.0 21.5 jit_solution(6176992889919253821)
XLA Ops:
  0.0 0.0 copy-start
  0.0 0.0 copy-start.1
  0.0 0.0 copy-start.2
  0.0 0.0 copy-start.3
  0.0 0.0 copy-start.4
  0.0 0.0 copy-start.5
  0.0 0.0 copy-start.7
  0.1 0.0 copy-start.8
  0.1 0.0 copy-start.9
  0.1 0.0 copy-start.10
  0.1 3.2 %shard_map.100 = (f32[16,128]{1,0:T(8,128)}, f32[16,128]{1,0:T(8,128)}) custom-call(s32[1,32]{1,0:T(1,128)} %live_ref.7, f32[128,2048]{1,0:T(8,128)} %bitcast.6, f32[128,2048]{1,0:T(8,128)} %bitcast.9, bf16[384,256]{1,0:T(8,128)(2,1)} %constant.2.clone.d_hbm.deriv), custom_call_target="tpu_custom_call" | custom-call | flops 4000000000 | bytes 100000 | tf_op jit(solution)/shard_map/pallas_call | solution.py:286
  3.3 2.0 %collective-permute-start.1 = (f32[16,128]{1,0:T(8,128)}, f32[16,128]{1,0:T(8,128)S(1)}, u32[]{:S(2)}, u32[]{:S(2)}) collective-permute-start(f32[16,128]{1,0:T(8,128)} %get-tuple-element.11), channel_id=1, source_target_pairs={{255,0},{0,1},{1,2},{2,3},{3,4},{4,5},{5,6},{6,7},{7,8},{8,9},{9,1... | collective-permute-start | bytes 24584 | tf_op jit(solution)/shard_map/ppermute | solution.py:259
  5.3 0.0 copy-done
  5.3 0.0 copy-done.1
  5.3 0.0 copy-done.2
  5.3 0.0 copy-done.3
  5.3 0.0 copy-done.4
  5.3 0.0 copy-done.5
  5.3 0.0 copy-done.7
  5.3 0.0 copy-done.8
  5.3 0.0 copy-done.9
  5.4 0.0 copy-done.10
  5.4 0.0 copy-start.6
  5.4 0.7 %copy-done.6 = f32[16,128]{1,0:T(8,128)S(1)} copy-done((f32[16,128]{1,0:T(8,128)S(1)}, f32[16,128]{1,0:T(8,128)}, u32[]{:S(2)}) %copy-start.6) | copy-done | bytes 8216
  6.1 5.3 %shard_map.101 = (f32[16,128]{1,0:T(8,128)S(1)}, f32[128,2048]{1,0:T(8,128)}) custom-call(s32[1,32]{1,0:T(1,128)S(1)} %copy-done.9, f32[16,128]{1,0:T(8,128)S(1)} %copy-done.6, f32[128,2048]{1,0:T(8,128)S(1)} %bitcast.7, f32[128,2048]{1,0:T(8,128)S(1)} %bitcast.10, bf16[128,1024]{1,0:T(8,128)(2,1)S(1)} %copy-done.3, f32[1,1024]{1,0:T(1,128)S(1)} %bitcast.12, ...), custom_call_target="tpu_custom_call" | custom-call | tf_op jit(solution)/shard_map/pallas_call | solution.py:298
  11.4 2.1 %collective-permute-start = (f32[16,128]{1,0:T(8,128)S(1)}, f32[16,128]{1,0:T(8,128)S(1)}, u32[]{:S(2)}, u32[]{:S(2)}) collective-permute-start(f32[16,128]{1,0:T(8,128)S(1)} %get-tuple-element.10), channel_id=1, source_target_pairs={{1,0},{2,1},{3,2},{4,3},{5,4},{6,5},{7,6},{8,7},{9,8},{10,9},{11,1... | collective-permute-start | bytes 24584 | tf_op jit(solution)/shard_map/ppermute | solution.py:259
  13.5 5.7 %shard_map.102.i_hbm = f32[128,2048]{1,0:T(8,128)} custom-call(s32[1,32]{1,0:T(1,128)S(1)} %copy-done.9, f32[128,2048]{1,0:T(8,128)S(1)} %bitcast.8, f32[128,2048]{1,0:T(8,128)S(1)} %bitcast.11, bf16[128,1024]{1,0:T(8,128)(2,1)S(1)} %copy-done.3, f32[1,1024]{1,0:T(1,128)S(1)} %bitcast.13, ...), custom_call_target="tpu_custom_call", output_to_operand_aliasing={{}: (10, {})} | custom-call | flops 6000000000 | bytes 6000000 | tf_op jit(solution)/shard_map/pallas_call | solution.py:307
  19.2 0.0 collective-permute-done.1.before_ref
  19.2 0.0 collective-permute-done.after_ref
  19.2 2.1 %shard_map.103 = f32[128,2048]{1,0:T(8,128)} custom-call(s32[1,32]{1,0:T(1,128)S(1)} %copy-done.9, f32[16,128]{1,0:T(8,128)S(1)} %collective-permute-done.after_ref, f32[16,128]{1,0:T(8,128)S(1)} %collective-permute-done.1.before_ref, f32[128,2048]{1,0:T(8,128)} %shard_map.102.i_hbm), custom_call_target="tpu_custom_call", output_to_operand_aliasing={{}: (3, {})} | custom-call | tf_op jit(solution)/shard_map/pallas_call | solution.py:319
Async XLA Ops:
  0.0 5.3 %copy-start = (bf16[1024,1024]{1,0:T(8,128)(2,1)S(1)}, bf16[1024,1024]{1,0:T(8,128)(2,1)}, u32[]{:S(2)}) copy-start(bf16[1024,1024]{1,0:T(8,128)(2,1)} %w2.3) | copy-start | bytes 6291460
  0.0 5.3 %copy-start.1 = (f32[2,64,2048]{2,1,0:T(8,128)S(1)}, f32[2,64,2048]{2,1,0:T(8,128)}, u32[]{:S(2)}) copy-start(f32[2,64,2048]{2,1,0:T(8,128)} %param.10) | copy-start | bytes 3145732
  0.0 5.3 %copy-start.2 = (f32[2,64,2048]{2,1,0:T(8,128)S(1)}, f32[2,64,2048]{2,1,0:T(8,128)}, u32[]{:S(2)}) copy-start(f32[2,64,2048]{2,1,0:T(8,128)} %param.11) | copy-start | bytes 3145732
  0.0 5.3 %copy-start.3 = (bf16[128,1024]{1,0:T(8,128)(2,1)S(1)}, bf16[128,1024]{1,0:T(8,128)(2,1)}, u32[]{:S(2)}) copy-start(bf16[128,1024]{1,0:T(8,128)(2,1)} %w1.3) | copy-start | bytes 786436
  0.0 5.3 %copy-start.4 = (bf16[1024,128]{1,0:T(8,128)(2,1)S(1)}, bf16[1024,128]{1,0:T(8,128)(2,1)}, u32[]{:S(2)}) copy-start(bf16[1024,128]{1,0:T(8,128)(2,1)} %w3.3) | copy-start | bytes 786436
  0.0 5.3 %copy-start.5 = (bf16[384,256]{1,0:T(8,128)(2,1)S(1)}, bf16[384,256]{1,0:T(8,128)(2,1)}, u32[]{:S(2)}) copy-start(bf16[384,256]{1,0:T(8,128)(2,1)} %constant.2.clone.d_hbm.deriv) | copy-start | bytes 589828
  0.0 5.3 %copy-start.7 = (f32[1024]{0:T(1024)S(1)}, f32[1024]{0:T(1024)}, u32[]{:S(2)}) copy-start(f32[1024]{0:T(1024)} %param.14) | copy-start | bytes 12292
  0.1 5.3 %copy-start.8 = (f32[1024]{0:T(1024)S(1)}, f32[1024]{0:T(1024)}, u32[]{:S(2)}) copy-start(f32[1024]{0:T(1024)} %param.16) | copy-start | bytes 12292
  0.1 5.3 %copy-start.9 = (s32[1,32]{1,0:T(1,128)S(1)}, s32[1,32]{1,0:T(1,128)}, u32[]{:S(2)}) copy-start(s32[1,32]{1,0:T(1,128)} %live_ref.7) | copy-start | bytes 388
  0.1 5.3 %copy-start.10 = (f32[128]{0:T(128)S(1)}, f32[128]{0:T(128)}, u32[]{:S(2)}) copy-start(f32[128]{0:T(128)} %param.18) | copy-start | bytes 1540
  3.3 15.9 %collective-permute-start.1 = (f32[16,128]{1,0:T(8,128)}, f32[16,128]{1,0:T(8,128)S(1)}, u32[]{:S(2)}, u32[]{:S(2)}) collective-permute-start(f32[16,128]{1,0:T(8,128)} %get-tuple-element.11), channel_id=1, source_target_pairs={{255,0},{0,1},{1,2},{2,3},{3,4},{4,5},{5,6},{6,7},{7,8},{8,9},{9,1... | collective-permute-start | bytes 24584 | tf_op jit(solution)/shard_map/ppermute | solution.py:259
  5.4 0.7 %copy-start.6 = (f32[16,128]{1,0:T(8,128)S(1)}, f32[16,128]{1,0:T(8,128)}, u32[]{:S(2)}) copy-start(f32[16,128]{1,0:T(8,128)} %get-tuple-element.9.first_ref) | copy-start | bytes 24580
  11.4 7.8 %collective-permute-start = (f32[16,128]{1,0:T(8,128)S(1)}, f32[16,128]{1,0:T(8,128)S(1)}, u32[]{:S(2)}, u32[]{:S(2)}) collective-permute-start(f32[16,128]{1,0:T(8,128)S(1)} %get-tuple-element.10), channel_id=1, source_target_pairs={{1,0},{2,1},{3,2},{4,3},{5,4},{6,5},{7,6},{8,7},{9,8},{10,9},{11,1... | collective-permute-start | bytes 24584 | tf_op jit(solution)/shard_map/ppermute | solution.py:259

commit v3 on v2

v3 whole, which is shorter than its diff:
```python
import functools

import jax
import jax.numpy as jnp
import numpy as np
from jax import lax
from jax.experimental import pallas as pl
from jax.experimental.pallas import tpu as pltpu
from jax.sharding import PartitionSpec as P

TIMESTEP = 0.1
LANES = 128
TILE = 512
HALF = 256
EARLY = ((6, 6, 4, 2, 2, 1, 1, 0), (2, 2, 2, 1, 1, 0, 0, 0))
CHUNK = 256
BF = jnp.bfloat16
F32 = jnp.float32
MIB = 2**20


def gll_table():
    points = np.array([-1.0, -1.0 / np.sqrt(5.0), 1.0 / np.sqrt(5.0), 1.0])
    legendre = 0.5 * (5.0 * points**3 - 3.0 * points)
    deriv_table = np.zeros((4, 4))
    for i in range(4):
        for j in range(4):
            if i != j:
                deriv_table[i, j] = legendre[i] / (legendre[j] * (points[i] - points[j]))
    deriv_table[0, 0] = -3.0
    deriv_table[3, 3] = 3.0
    return deriv_table


def deriv_operand():
    deriv_table = gll_table()
    along_xi = np.kron(np.eye(8), np.kron(np.eye(4), deriv_table)).T
    along_eta = np.kron(np.eye(8), np.kron(deriv_table, np.eye(4))).T
    both = np.concatenate([along_xi, along_eta], axis=1).astype(np.float32)
    high = both.astype(jnp.bfloat16)
    low = (both - high.astype(np.float32)).astype(jnp.bfloat16)
    return jnp.asarray(np.concatenate([high, high, low], axis=0))


def block_rate(s, wind_xi, wind_eta, deriv):
    high = s.astype(BF)
    low = (s - high.astype(F32)).astype(BF)
    d = jnp.dot(
        jnp.concatenate([high, low, high], axis=1), deriv, preferred_element_type=F32
    )
    return -(wind_xi * d[:, :LANES] + wind_eta * d[:, LANES:])


def both_fields(w):
    return jnp.concatenate([w, w], axis=0)


def lane_ids():
    return lax.broadcasted_iota(jnp.int32, (LANES, LANES), 1)


def own_live(live_ref):
    return live_ref[0, lax.axis_index("col")] * 16


def early_tiles():
    col = lax.axis_index("col")
    amount = 0
    for z in range(8):
        here = jnp.where(col // 8 == 0, EARLY[0][z], EARLY[1][z])
        amount = jnp.where(col % 8 == z, here, amount)
    return amount


def fetch(source, target, sems, index):
    copy = pltpu.make_async_copy(source, target, sems.at[index])
    copy.start()
    return copy


def last_block(count):
    return pl.multiple_of((count - 16) // LANES * LANES, LANES)


def edge_of(rate, lanes_back, row):
    turn = jnp.where(lanes_back > 0, LANES - lanes_back, 0)
    turned = pltpu.roll(rate, turn, 1).T[0:16]
    rows = lax.broadcasted_iota(jnp.int32, (16, LANES), 0)
    return jnp.where(rows % 4 == row, turned, 0.0)


def first_layer(at, s_v, w1, b1, h1, size):
    units = h1.shape[1]
    x = s_v[:, at : at + size].astype(BF)
    for n in range(0, units, CHUNK):
        a = lax.dot_general(
            x, w1[:, n : n + CHUNK], (((0,), (0,)), ((), ())), preferred_element_type=F32
        )
        h1[at : at + size, n : n + CHUNK] = jax.nn.silu(a + b1[:, n : n + CHUNK]).astype(BF)


def rate_at(block, s_v, w_v, deriv, rate, slot):
    cols = pl.ds(pl.multiple_of(block * LANES, LANES), LANES)
    rate[:, pl.ds(pl.multiple_of(slot * LANES + LANES, LANES), LANES)] = block_rate(
        s_v[:, cols], both_fields(w_v[0:64, cols]), both_fields(w_v[64:128, cols]), deriv[...]
    )


def finish_tile(at, count, s_v, w2, b2, w3t, b3_rows, h1, h2, rate, o_v, size):
    units = h1.shape[1]
    h = h1[at : at + size, :]
    for n in range(0, units, CHUNK):
        a = jnp.dot(h, w2[:, n : n + CHUNK], preferred_element_type=F32)
        h2[0:size, n : n + CHUNK] = jax.nn.silu(a + b2[:, n : n + CHUNK]).astype(BF)
    third = lax.dot_general(
        w3t[...], h2[0:size], (((1,), (1,)), ((), ())), preferred_element_type=F32
    )
    lanes = lane_ids()
    for k in range(0, size, LANES):
        base = at + k
        own = rate[:, pl.ds(base + LANES, LANES)]
        after = rate[:, pl.ds(base + 2 * LANES, LANES)]
        prior = rate[:, pl.ds(base, LANES)]
        ids = lanes + base
        east = pltpu.roll(jnp.where(lanes < 13, after, own), LANES - 13, 1)
        west = pltpu.roll(jnp.where(lanes >= LANES - 13, prior, own), 13, 1)
        east = jnp.where(ids < count - 16, east, 0.0)
        west = jnp.where(ids >= 16, west, 0.0)
        twin = jnp.where(lanes % 4 == 3, east, jnp.where(lanes % 4 == 0, west, own))
        tendency = (third[:, k : k + LANES] + b3_rows[...]).astype(BF).astype(F32)
        value = s_v[:, pl.ds(base, LANES)] + (0.5 * TIMESTEP) * (own + twin) + tendency
        o_v[:, pl.ds(base, LANES)] = jnp.where(ids < count, value, 0.0)


def ready_last(w3, b3, w3t, b3_rows):
    w3t[...] = w3[...].T
    b3_rows[...] = jnp.broadcast_to(b3[...], (LANES, LANES)).T


def do_tiles(begin, end, count, refs, held_ref, o_hbm, sem):
    s_v, w1, b1, w2, b2, w3, b3, deriv, w_v, w3t, b3_rows, h1, h2, rate, o_v = refs
    spans = [(begin, 1)] if (end - begin) % 2 else []
    spans += [(at, 2) for at in range(begin + len(spans), end, 2)]
    spans = [(at * HALF, size * HALF) for at, size in spans]
    for at, size in spans:
        first_layer(at, s_v, w1, b1, h1, size)
    ready_last(w3, b3, w3t, b3_rows)
    blocks = s_v.shape[1] // LANES
    per = HALF // LANES
    for block in range(max(begin * per - 1, 0), min(end * per + 1, blocks)):
        rate_at(block, s_v, w_v, deriv, rate, block)
    copies = []
    for at, size in spans:
        finish_tile(at, count, s_v, w2, b2, w3t, b3_rows, h1, h2, rate, o_v, size)
        cols = pl.ds(at, size)
        copies.append(pltpu.make_async_copy(o_v.at[:, cols], o_hbm.at[:, cols], sem))
        copies[-1].start()
    if begin == 0:
        held_ref[0] = o_v[:, 0:LANES]
    held_ref[1] = o_v[:, pl.ds(last_block(count), LANES)]
    for copy in copies:
        copy.wait()


def edge_kernel(live_ref, s_hbm, w_hbm, d_hbm, last_ref, s_e, w_e, deriv, sems):
    start = own_live(live_ref) - 16
    block = pl.multiple_of(start // LANES * LANES, LANES)
    copies = [
        fetch(s_hbm.at[:, pl.ds(block, LANES)], s_e, sems, 0),
        fetch(w_hbm.at[:, pl.ds(block, LANES)], w_e, sems, 1),
        fetch(d_hbm, deriv, sems, 2),
    ]
    for copy in copies:
        copy.wait()
    rate = block_rate(s_e[...], both_fields(w_e[0:64]), both_fields(w_e[64:128]), deriv[...])
    last_ref[...] = edge_of(rate, start - block + 3, 0)


def early_kernel(
    live_ref, last_ref, s_v, w_v, w1, b1, w2, b2, w3, b3, deriv, first_ref, held_ref, o_hbm,
    w3t, b3_rows, h1, h2, rate, o_v, sems,
):
    del last_ref
    rate_at(0, s_v, w_v, deriv, rate, 0)
    first_ref[...] = edge_of(rate[:, LANES : 2 * LANES], LANES - 3, 3)
    early = early_tiles()
    refs = [s_v, w1, b1, w2, b2, w3, b3, deriv, w_v, w3t, b3_rows, h1, h2, rate, o_v]
    for amount in sorted(set(EARLY[0] + EARLY[1]) - {0}):

        @pl.when(early == amount)
        def _():
            do_tiles(0, amount, own_live(live_ref), refs, held_ref, o_hbm, sems.at[0])


def late_kernel(
    live_ref, s_v, w_v, w1, b1, w2, b2, w3, b3, deriv, i_hbm, held_ref, o_hbm,
    w3t, b3_rows, h1, h2, rate, o_v, sems,
):
    del i_hbm
    early = early_tiles()
    refs = [s_v, w1, b1, w2, b2, w3, b3, deriv, w_v, w3t, b3_rows, h1, h2, rate, o_v]
    tiles = s_v.shape[1] // HALF
    for amount in sorted(set(EARLY[0] + EARLY[1]) | {0}):

        @pl.when(early == amount)
        def _():
            do_tiles(amount, tiles, own_live(live_ref), refs, held_ref, o_hbm, sems.at[0])


def twin_kernel(
    live_ref, after_ref, before_ref, early_ref, late_ref, i_hbm, o_hbm, held, sems
):
    del i_hbm
    count = own_live(live_ref)
    block = last_block(count)
    border = early_tiles() * HALF
    pad = jnp.zeros((LANES - 16, LANES), F32)
    half = 0.5 * TIMESTEP
    west = half * jnp.concatenate([before_ref[...], pad], axis=0).T
    east = half * pltpu.roll(
        jnp.concatenate([after_ref[...], pad], axis=0).T, count - 16 - block, 1
    )
    shared = block == 0
    begun = jnp.where(border > 0, early_ref[0], late_ref[0])
    ended = jnp.where(block < border, early_ref[1], late_ref[1])
    held[0] = begun + west + jnp.where(shared, east, 0.0)
    held[1] = ended + east
    stores = [
        pltpu.make_async_copy(held.at[0], o_hbm.at[:, pl.ds(0, LANES)], sems.at[0]),
        pltpu.make_async_copy(held.at[1], o_hbm.at[:, pl.ds(block, LANES)], sems.at[1]),
    ]
    stores[0].start()

    @pl.when(block > 0)
    def _():
        stores[1].start()
        stores[1].wait()

    stores[0].wait()


def passed_along(block, axis, distance):
    devices = range(lax.axis_size(axis))
    route = [((i - distance) % len(devices), i) for i in devices]
    return lax.ppermute(block, axis, route)


def body(state, wind, live, w_first, b_first, w_second, b_second, w_third, b_third):
    fields, levels, columns = state.shape
    features = fields * levels
    units = w_first.shape[1]
    s = state.reshape(features, columns)
    w = wind.reshape(features, columns)
    deriv = deriv_operand()
    smem = pl.BlockSpec(memory_space=pltpu.SMEM)
    vmem = pl.BlockSpec(memory_space=pltpu.VMEM)
    hbm = pl.BlockSpec(memory_space=pltpu.HBM)
    edge = jax.ShapeDtypeStruct((16, LANES), F32)
    whole = jax.ShapeDtypeStruct((features, columns), F32)
    operands = [
        s, w, w_first, b_first[None], w_second, b_second[None], w_third, b_third[None], deriv
    ]
    work = [
        pltpu.VMEM((LANES, units), BF),
        pltpu.VMEM((LANES, LANES), F32),
        pltpu.VMEM((columns, units), BF),
        pltpu.VMEM((TILE, units), BF),
        pltpu.VMEM((features, columns + 2 * LANES), F32),
        pltpu.VMEM((features, columns), F32),
    ]
    pair = pltpu.VMEM((2, features, LANES), F32)
    pair_out = jax.ShapeDtypeStruct((2, features, LANES), F32)
    block = pltpu.VMEM((features, LANES), F32)
    last = pl.pallas_call(
        edge_kernel,
        out_shape=edge,
        in_specs=[smem, hbm, hbm, hbm],
        out_specs=vmem,
        scratch_shapes=[block, block, pltpu.VMEM(deriv.shape, BF), pltpu.SemaphoreType.DMA((3,))],
        compiler_params=pltpu.CompilerParams(vmem_limit_bytes=54 * MIB - 128 * 1024),
        cost_estimate=pl.CostEstimate(flops=4 * 10**9, bytes_accessed=10**5, transcendentals=0),
    )(live, s, w, deriv)
    before = passed_along(last, ("grp", "col"), 1)
    work.append(pltpu.SemaphoreType.DMA((1,)))
    params = pltpu.CompilerParams(vmem_limit_bytes=28 * MIB)
    first, held, out = pl.pallas_call(
        early_kernel,
        out_shape=(edge, pair_out, whole),
        in_specs=[smem, vmem] + [vmem] * len(operands),
        out_specs=(vmem, vmem, hbm),
        scratch_shapes=work,
        compiler_params=params,
    )(live, last, *operands)
    after = passed_along(first, ("grp", "col"), -1)
    rest, out = pl.pallas_call(
        late_kernel,
        out_shape=(pair_out, whole),
        in_specs=[smem] + [vmem] * len(operands) + [hbm],
        out_specs=(vmem, hbm),
        scratch_shapes=work,
        input_output_aliases={1 + len(operands): 1},
        compiler_params=params,
        cost_estimate=pl.CostEstimate(
            flops=6 * 10**9, bytes_accessed=6 * 10**6, transcendentals=4 * 10**6
        ),
    )(live, *operands, out)
    out = pl.pallas_call(
        twin_kernel,
        out_shape=whole,
        in_specs=[smem] + [vmem] * 4 + [hbm],
        out_specs=hbm,
        scratch_shapes=[pair, pltpu.SemaphoreType.DMA((2,))],
        input_output_aliases={5: 0},
        compiler_params=pltpu.CompilerParams(vmem_limit_bytes=2 * MIB),
    )(live, after, before, held, rest, out)
    return out.reshape(fields, levels, columns)


def solution(mesh):
    return jax.shard_map(
        body,
        mesh=mesh,
        in_specs=(
            P(None, None, ("grp", "col")),
            P(None, None, ("grp", "col")),
            P("grp", None),
            P(),
            P(),
            P(),
            P(),
            P(),
            P(),
        ),
        out_specs=P(None, None, ("grp", "col")),
        check_vma=False,
    )
```

time: 21.7 us -> 20.9 us (0.963)
  the two profiles are of different devices: /device:TPU:40 before, /device:TPU:80 now
where the time goes in v3:
time: 20.9 us; the launch traced here: 20.8 us
  Pallas kernels  15.5 us (74%)
  starting transfers between devices  4.3 us (21%)
  local copies, waits for them, and re-layouts  0.69 us (3%)
  between operations  0.35 us (2%)
    pallas_call x1, Pallas kernels, body(): pl.pallas_call(late_kernel, out_shape=(pair_out, whole), in_specs=[smem]...  6.21 us
    pallas_call x1, Pallas kernels, body(): pl.pallas_call(early_kernel, out_shape=(edge, pair_out, whole), in_specs=...  5.69 us
    ppermute x2, starting transfers between devices, passed_along(): return lax.ppermute(block, axis, route)  4.3 us
    pallas_call x1, Pallas kernels, body(): pl.pallas_call(edge_kernel, out_shape=edge, in_specs=[smem, hbm, hbm, hbm...  2.18 us
    pallas_call x1, Pallas kernels, body(): pl.pallas_call(twin_kernel, out_shape=whole, in_specs=[smem] + [vmem] * 4...  1.38 us
    unnamed x20, local copies, waits for them, and re-layouts  0.69 us
  transfers between devices with their start and end apart: 2, of which 0 were waited for; matrix products, arithmetic and copies ran while one was open for 0% of the time, Pallas kernels for 57%

profile of v3, /device:TPU:80, one launch (start us, length us, event | category | flops | bytes accessed | tf_op | source)
XLA Modules:
  0.0 20.8 jit_solution(16274139599152072454)
XLA Ops:
  0.0 0.0 copy-start.8
  0.0 0.7 %copy-done.8 = s32[1,32]{1,0:T(1,128)S(1)} copy-done((s32[1,32]{1,0:T(1,128)S(1)}, s32[1,32]{1,0:T(1,128)}, u32[]{:S(2)}) %copy-start.8) | copy-done | bytes 152
  0.7 0.0 copy-start
  0.7 0.0 copy-start.1
  0.7 0.0 copy-start.2
  0.7 0.0 copy-start.3
  0.7 0.0 copy-start.4
  0.7 0.0 copy-start.5
  0.7 0.0 copy-start.6
  0.7 0.0 copy-start.7
  0.7 0.0 copy-start.9
  0.7 2.2 %shard_map.100.last_ref = f32[16,128]{1,0:T(8,128)S(1)} custom-call(s32[1,32]{1,0:T(1,128)S(1)} %copy-done.8, f32[128,2048]{1,0:T(8,128)} %bitcast.6, f32[128,2048]{1,0:T(8,128)} %bitcast.9, bf16[384,256]{1,0:T(8,128)(2,1)} %constant.2.clone.d_hbm.deriv), custom_call_target="tpu_custom_call" | custom-call | flops 4000000000 | bytes 100000 | tf_op jit(solution)/shard_map/pallas_call | solution.py:274
  2.9 2.0 %collective-permute-start.1 = (f32[16,128]{1,0:T(8,128)S(1)}, f32[16,128]{1,0:T(8,128)S(1)}, u32[]{:S(2)}, u32[]{:S(2)}) collective-permute-start(f32[16,128]{1,0:T(8,128)S(1)} %shard_map.100.last_ref), channel_id=1, source_target_pairs={{255,0},{0,1},{1,2},{2,3},{3,4},{4,5},{5,6},{6,7},{7,8},{8,9},{9,1... | collective-permute-start | bytes 24584 | tf_op jit(solution)/shard_map/ppermute | solution.py:245
  4.9 0.0 copy-done
  4.9 0.0 copy-done.1
  4.9 0.0 copy-done.2
  4.9 0.0 copy-done.3
  4.9 0.0 copy-done.4
  4.9 0.0 copy-done.5
  4.9 0.0 copy-done.6
  4.9 0.0 copy-done.7
  5.0 0.0 copy-done.9
  5.0 5.7 %shard_map.101 = (f32[16,128]{1,0:T(8,128)S(1)}, f32[2,128,128]{2,1,0:T(8,128)S(1)}, f32[128,2048]{1,0:T(8,128)}) custom-call(s32[1,32]{1,0:T(1,128)S(1)} %copy-done.8, f32[16,128]{1,0:T(8,128)S(1)} %shard_map.100.last_ref, f32[128,2048]{1,0:T(8,128)S(1)} %bitcast.7, f32[128,2048]{1,0:T(8,128)S(1)} %bitcast.10, bf16[128,1024]{1,0:T(8,128)(2,1)S(1)} %copy-done.3, ...), custom_call_target="tpu_custom_call" | custom-call | tf_op jit(solution)/shard_map/pallas_call | solution.py:286
  10.7 2.3 %collective-permute-start = (f32[16,128]{1,0:T(8,128)S(1)}, f32[16,128]{1,0:T(8,128)S(1)}, u32[]{:S(2)}, u32[]{:S(2)}) collective-permute-start(f32[16,128]{1,0:T(8,128)S(1)} %get-tuple-element.10), channel_id=1, source_target_pairs={{1,0},{2,1},{3,2},{4,3},{5,4},{6,5},{7,6},{8,7},{9,8},{10,9},{11,1... | collective-permute-start | bytes 24584 | tf_op jit(solution)/shard_map/ppermute | solution.py:245
  13.0 6.2 %shard_map.102 = (f32[2,128,128]{2,1,0:T(8,128)S(1)}, f32[128,2048]{1,0:T(8,128)}) custom-call(s32[1,32]{1,0:T(1,128)S(1)} %copy-done.8, f32[128,2048]{1,0:T(8,128)S(1)} %bitcast.8, f32[128,2048]{1,0:T(8,128)S(1)} %bitcast.11, bf16[128,1024]{1,0:T(8,128)(2,1)S(1)} %copy-done.3, f32[1,1024]{1,0:T(1,128)S(1)} %bitcast.13, ...), custom_call_target="tpu_custom_call", output_to_operand_aliasing={{1}: (10, {})} | custom-call | flops 6000000000 | bytes 6000000 | tf_op jit(solution)/shard_map/pallas_call | solution.py:295
  19.2 0.0 collective-permute-done.1.before_ref
  19.2 0.0 collective-permute-done.after_ref
  19.2 1.4 %shard_map.103 = f32[128,2048]{1,0:T(8,128)} custom-call(s32[1,32]{1,0:T(1,128)S(1)} %copy-done.8, f32[16,128]{1,0:T(8,128)S(1)} %collective-permute-done.after_ref, f32[16,128]{1,0:T(8,128)S(1)} %collective-permute-done.1.before_ref, f32[2,128,128]{2,1,0:T(8,128)S(1)} %get-tuple-element.11.early_ref, ...), custom_call_target="tpu_custom_call", output_to_operand_aliasing={{}: (5, {})} | custom-call | tf_op jit(solution)/shard_map/pallas_call | solution.py:307
Async XLA Ops:
  0.0 0.7 %copy-start.8 = (s32[1,32]{1,0:T(1,128)S(1)}, s32[1,32]{1,0:T(1,128)}, u32[]{:S(2)}) copy-start(s32[1,32]{1,0:T(1,128)} %live_ref.7) | copy-start | bytes 388
  0.7 4.2 %copy-start = (bf16[1024,1024]{1,0:T(8,128)(2,1)S(1)}, bf16[1024,1024]{1,0:T(8,128)(2,1)}, u32[]{:S(2)}) copy-start(bf16[1024,1024]{1,0:T(8,128)(2,1)} %w2.3) | copy-start | bytes 6291460
  0.7 4.2 %copy-start.1 = (f32[2,64,2048]{2,1,0:T(8,128)S(1)}, f32[2,64,2048]{2,1,0:T(8,128)}, u32[]{:S(2)}) copy-start(f32[2,64,2048]{2,1,0:T(8,128)} %param.10) | copy-start | bytes 3145732
  0.7 4.2 %copy-start.2 = (f32[2,64,2048]{2,1,0:T(8,128)S(1)}, f32[2,64,2048]{2,1,0:T(8,128)}, u32[]{:S(2)}) copy-start(f32[2,64,2048]{2,1,0:T(8,128)} %param.11) | copy-start | bytes 3145732
  0.7 4.2 %copy-start.3 = (bf16[128,1024]{1,0:T(8,128)(2,1)S(1)}, bf16[128,1024]{1,0:T(8,128)(2,1)}, u32[]{:S(2)}) copy-start(bf16[128,1024]{1,0:T(8,128)(2,1)} %w1.3) | copy-start | bytes 786436
  0.7 4.2 %copy-start.4 = (bf16[1024,128]{1,0:T(8,128)(2,1)S(1)}, bf16[1024,128]{1,0:T(8,128)(2,1)}, u32[]{:S(2)}) copy-start(bf16[1024,128]{1,0:T(8,128)(2,1)} %w3.3) | copy-start | bytes 786436
  0.7 4.2 %copy-start.5 = (bf16[384,256]{1,0:T(8,128)(2,1)S(1)}, bf16[384,256]{1,0:T(8,128)(2,1)}, u32[]{:S(2)}) copy-start(bf16[384,256]{1,0:T(8,128)(2,1)} %constant.2.clone.d_hbm.deriv) | copy-start | bytes 589828
  0.7 4.2 %copy-start.6 = (f32[1024]{0:T(1024)S(1)}, f32[1024]{0:T(1024)}, u32[]{:S(2)}) copy-start(f32[1024]{0:T(1024)} %param.14) | copy-start | bytes 12292
  0.7 4.2 %copy-start.7 = (f32[1024]{0:T(1024)S(1)}, f32[1024]{0:T(1024)}, u32[]{:S(2)}) copy-start(f32[1024]{0:T(1024)} %param.16) | copy-start | bytes 12292
  0.7 4.2 %copy-start.9 = (f32[128]{0:T(128)S(1)}, f32[128]{0:T(128)}, u32[]{:S(2)}) copy-start(f32[128]{0:T(128)} %param.18) | copy-start | bytes 1540
  2.9 16.3 %collective-permute-start.1 = (f32[16,128]{1,0:T(8,128)S(1)}, f32[16,128]{1,0:T(8,128)S(1)}, u32[]{:S(2)}, u32[]{:S(2)}) collective-permute-start(f32[16,128]{1,0:T(8,128)S(1)} %shard_map.100.last_ref), channel_id=1, source_target_pairs={{255,0},{0,1},{1,2},{2,3},{3,4},{4,5},{5,6},{6,7},{7,8},{8,9},{9,1... | collective-permute-start | bytes 24584 | tf_op jit(solution)/shard_map/ppermute | solution.py:245
  10.7 8.5 %collective-permute-start = (f32[16,128]{1,0:T(8,128)S(1)}, f32[16,128]{1,0:T(8,128)S(1)}, u32[]{:S(2)}, u32[]{:S(2)}) collective-permute-start(f32[16,128]{1,0:T(8,128)S(1)} %get-tuple-element.10), channel_id=1, source_target_pairs={{1,0},{2,1},{3,2},{4,3},{5,4},{6,5},{7,6},{8,7},{9,8},{10,9},{11,1... | collective-permute-start | bytes 24584 | tf_op jit(solution)/shard_map/ppermute | solution.py:245

commit v4 on v3

--- a/solution.py
+++ b/solution.py
@@ -12,7 +12,7 @@
 LANES = 128
 TILE = 512
 HALF = 256
-EARLY = ((6, 6, 4, 2, 2, 1, 1, 0), (2, 2, 2, 1, 1, 0, 0, 0))
+EARLY = ((6, 6, 6, 4, 4, 2, 1, 0), (2, 2, 2, 1, 1, 0, 0, 0))
 CHUNK = 256
 BF = jnp.bfloat16
 F32 = jnp.float32

time: 20.9 us -> 20.9 us (level)
  the two profiles are of different devices: /device:TPU:80 before, /device:TPU:104 now
where the time goes in v4:
time: 20.9 us; the launch traced here: 20.8 us
  Pallas kernels  15.5 us (74%)
  starting transfers between devices  4.3 us (21%)
  local copies, waits for them, and re-layouts  0.69 us (3%)
  between operations  0.35 us (2%)
    pallas_call x1, Pallas kernels, body(): pl.pallas_call(late_kernel, out_shape=(pair_out, whole), in_specs=[smem]...  6.23 us
    pallas_call x1, Pallas kernels, body(): pl.pallas_call(early_kernel, out_shape=(edge, pair_out, whole), in_specs=...  5.69 us
    ppermute x2, starting transfers between devices, passed_along(): return lax.ppermute(block, axis, route)  4.3 us
    pallas_call x1, Pallas kernels, body(): pl.pallas_call(edge_kernel, out_shape=edge, in_specs=[smem, hbm, hbm, hbm...  2.18 us
    pallas_call x1, Pallas kernels, body(): pl.pallas_call(twin_kernel, out_shape=whole, in_specs=[smem] + [vmem] * 4...  1.38 us
    unnamed x20, local copies, waits for them, and re-layouts  0.69 us
  transfers between devices with their start and end apart: 2, of which 0 were waited for; matrix products, arithmetic and copies ran while one was open for 0% of the time, Pallas kernels for 57%

profile of v4, /device:TPU:104, one launch (start us, length us, event | category | flops | bytes accessed | tf_op | source)
XLA Modules:
  0.0 20.8 jit_solution(6360810735474080197)
XLA Ops:
  0.0 0.0 copy-start.8
  0.0 0.7 %copy-done.8 = s32[1,32]{1,0:T(1,128)S(1)} copy-done((s32[1,32]{1,0:T(1,128)S(1)}, s32[1,32]{1,0:T(1,128)}, u32[]{:S(2)}) %copy-start.8) | copy-done | bytes 152
  0.7 0.0 copy-start
  0.7 0.0 copy-start.1
  0.7 0.0 copy-start.2
  0.7 0.0 copy-start.3
  0.7 0.0 copy-start.4
  0.7 0.0 copy-start.5
  0.7 0.0 copy-start.6
  0.7 0.0 copy-start.7
  0.7 0.0 copy-start.9
  0.7 2.2 %shard_map.100.last_ref = f32[16,128]{1,0:T(8,128)S(1)} custom-call(s32[1,32]{1,0:T(1,128)S(1)} %copy-done.8, f32[128,2048]{1,0:T(8,128)} %bitcast.6, f32[128,2048]{1,0:T(8,128)} %bitcast.9, bf16[384,256]{1,0:T(8,128)(2,1)} %constant.2.clone.d_hbm.deriv), custom_call_target="tpu_custom_call" | custom-call | flops 4000000000 | bytes 100000 | tf_op jit(solution)/shard_map/pallas_call | solution.py:274
  2.9 3.2 %collective-permute-start.1 = (f32[16,128]{1,0:T(8,128)S(1)}, f32[16,128]{1,0:T(8,128)S(1)}, u32[]{:S(2)}, u32[]{:S(2)}) collective-permute-start(f32[16,128]{1,0:T(8,128)S(1)} %shard_map.100.last_ref), channel_id=1, source_target_pairs={{255,0},{0,1},{1,2},{2,3},{3,4},{4,5},{5,6},{6,7},{7,8},{8,9},{9,1... | collective-permute-start | bytes 24584 | tf_op jit(solution)/shard_map/ppermute | solution.py:245
  6.1 0.0 copy-done
  6.1 0.0 copy-done.1
  6.1 0.0 copy-done.2
  6.1 0.0 copy-done.3
  6.1 0.0 copy-done.4
  6.1 0.0 copy-done.5
  6.1 0.0 copy-done.6
  6.2 0.0 copy-done.7
  6.2 0.0 copy-done.9
  6.2 5.7 %shard_map.101 = (f32[16,128]{1,0:T(8,128)S(1)}, f32[2,128,128]{2,1,0:T(8,128)S(1)}, f32[128,2048]{1,0:T(8,128)}) custom-call(s32[1,32]{1,0:T(1,128)S(1)} %copy-done.8, f32[16,128]{1,0:T(8,128)S(1)} %shard_map.100.last_ref, f32[128,2048]{1,0:T(8,128)S(1)} %bitcast.7, f32[128,2048]{1,0:T(8,128)S(1)} %bitcast.10, bf16[128,1024]{1,0:T(8,128)(2,1)S(1)} %copy-done.3, ...), custom_call_target="tpu_custom_call" | custom-call | tf_op jit(solution)/shard_map/pallas_call | solution.py:286
  11.9 1.1 %collective-permute-start = (f32[16,128]{1,0:T(8,128)S(1)}, f32[16,128]{1,0:T(8,128)S(1)}, u32[]{:S(2)}, u32[]{:S(2)}) collective-permute-start(f32[16,128]{1,0:T(8,128)S(1)} %get-tuple-element.10), channel_id=1, source_target_pairs={{1,0},{2,1},{3,2},{4,3},{5,4},{6,5},{7,6},{8,7},{9,8},{10,9},{11,1... | collective-permute-start | bytes 24584 | tf_op jit(solution)/shard_map/ppermute | solution.py:245
  13.0 6.2 %shard_map.102 = (f32[2,128,128]{2,1,0:T(8,128)S(1)}, f32[128,2048]{1,0:T(8,128)}) custom-call(s32[1,32]{1,0:T(1,128)S(1)} %copy-done.8, f32[128,2048]{1,0:T(8,128)S(1)} %bitcast.8, f32[128,2048]{1,0:T(8,128)S(1)} %bitcast.11, bf16[128,1024]{1,0:T(8,128)(2,1)S(1)} %copy-done.3, f32[1,1024]{1,0:T(1,128)S(1)} %bitcast.13, ...), custom_call_target="tpu_custom_call", output_to_operand_aliasing={{1}: (10, {})} | custom-call | flops 6000000000 | bytes 6000000 | tf_op jit(solution)/shard_map/pallas_call | solution.py:295
  19.2 0.0 collective-permute-done.1.before_ref
  19.2 0.0 collective-permute-done.after_ref
  19.2 1.4 %shard_map.103 = f32[128,2048]{1,0:T(8,128)} custom-call(s32[1,32]{1,0:T(1,128)S(1)} %copy-done.8, f32[16,128]{1,0:T(8,128)S(1)} %collective-permute-done.after_ref, f32[16,128]{1,0:T(8,128)S(1)} %collective-permute-done.1.before_ref, f32[2,128,128]{2,1,0:T(8,128)S(1)} %get-tuple-element.11.early_ref, ...), custom_call_target="tpu_custom_call", output_to_operand_aliasing={{}: (5, {})} | custom-call | tf_op jit(solution)/shard_map/pallas_call | solution.py:307
Async XLA Ops:
  0.0 0.7 %copy-start.8 = (s32[1,32]{1,0:T(1,128)S(1)}, s32[1,32]{1,0:T(1,128)}, u32[]{:S(2)}) copy-start(s32[1,32]{1,0:T(1,128)} %live_ref.7) | copy-start | bytes 388
  0.7 5.5 %copy-start = (bf16[1024,1024]{1,0:T(8,128)(2,1)S(1)}, bf16[1024,1024]{1,0:T(8,128)(2,1)}, u32[]{:S(2)}) copy-start(bf16[1024,1024]{1,0:T(8,128)(2,1)} %w2.3) | copy-start | bytes 6291460
  0.7 5.5 %copy-start.1 = (f32[2,64,2048]{2,1,0:T(8,128)S(1)}, f32[2,64,2048]{2,1,0:T(8,128)}, u32[]{:S(2)}) copy-start(f32[2,64,2048]{2,1,0:T(8,128)} %param.10) | copy-start | bytes 3145732
  0.7 5.5 %copy-start.2 = (f32[2,64,2048]{2,1,0:T(8,128)S(1)}, f32[2,64,2048]{2,1,0:T(8,128)}, u32[]{:S(2)}) copy-start(f32[2,64,2048]{2,1,0:T(8,128)} %param.11) | copy-start | bytes 3145732
  0.7 5.5 %copy-start.3 = (bf16[128,1024]{1,0:T(8,128)(2,1)S(1)}, bf16[128,1024]{1,0:T(8,128)(2,1)}, u32[]{:S(2)}) copy-start(bf16[128,1024]{1,0:T(8,128)(2,1)} %w1.3) | copy-start | bytes 786436
  0.7 5.5 %copy-start.4 = (bf16[1024,128]{1,0:T(8,128)(2,1)S(1)}, bf16[1024,128]{1,0:T(8,128)(2,1)}, u32[]{:S(2)}) copy-start(bf16[1024,128]{1,0:T(8,128)(2,1)} %w3.3) | copy-start | bytes 786436
  0.7 5.5 %copy-start.5 = (bf16[384,256]{1,0:T(8,128)(2,1)S(1)}, bf16[384,256]{1,0:T(8,128)(2,1)}, u32[]{:S(2)}) copy-start(bf16[384,256]{1,0:T(8,128)(2,1)} %constant.2.clone.d_hbm.deriv) | copy-start | bytes 589828
  0.7 5.5 %copy-start.6 = (f32[1024]{0:T(1024)S(1)}, f32[1024]{0:T(1024)}, u32[]{:S(2)}) copy-start(f32[1024]{0:T(1024)} %param.14) | copy-start | bytes 12292
  0.7 5.5 %copy-start.7 = (f32[1024]{0:T(1024)S(1)}, f32[1024]{0:T(1024)}, u32[]{:S(2)}) copy-start(f32[1024]{0:T(1024)} %param.16) | copy-start | bytes 12292
  0.7 5.5 %copy-start.9 = (f32[128]{0:T(128)S(1)}, f32[128]{0:T(128)}, u32[]{:S(2)}) copy-start(f32[128]{0:T(128)} %param.18) | copy-start | bytes 1540
  2.9 16.3 %collective-permute-start.1 = (f32[16,128]{1,0:T(8,128)S(1)}, f32[16,128]{1,0:T(8,128)S(1)}, u32[]{:S(2)}, u32[]{:S(2)}) collective-permute-start(f32[16,128]{1,0:T(8,128)S(1)} %shard_map.100.last_ref), channel_id=1, source_target_pairs={{255,0},{0,1},{1,2},{2,3},{3,4},{4,5},{5,6},{6,7},{7,8},{8,9},{9,1... | collective-permute-start | bytes 24584 | tf_op jit(solution)/shard_map/ppermute | solution.py:245
  11.9 7.3 %collective-permute-start = (f32[16,128]{1,0:T(8,128)S(1)}, f32[16,128]{1,0:T(8,128)S(1)}, u32[]{:S(2)}, u32[]{:S(2)}) collective-permute-start(f32[16,128]{1,0:T(8,128)S(1)} %get-tuple-element.10), channel_id=1, source_target_pairs={{1,0},{2,1},{3,2},{4,3},{5,4},{6,5},{7,6},{8,7},{9,8},{10,9},{11,1... | collective-permute-start | bytes 24584 | tf_op jit(solution)/shard_map/ppermute | solution.py:245
